TPU v7x, 128 devices: a whole 4x4x4 slice. The times are simulated.
128 devices in a mesh: dp: 4 (over x_hi, core), space: 32 (over x_lo, y, z).
Axes of the slice: x: 4 (x_hi: 2, x_lo: 2; x = x_hi * 2 + x_lo), y: 4, z: 4, core: 2. Of those that a mesh axis runs over, the one named last changes fastest.
Arguments:
- samples: bfloat16 [4, 320, 720, 512], P('dp', 'space'), may hold values from -6 to 6
- norm_gain: float32 [512], replicated, may hold values from 0.1 to 1.9
- norm_bias: float32 [512], replicated, may hold values from -3 to 3
- spectral_filter: float32 [320, 512, 722], P(None, ('dp', 'space')), may hold values from -4.5 to 4.5
Outputs:
- updated: bfloat16 [4, 320, 720, 512], P('dp', 'space')
All inputs are finite; a program needn't handle non-finite values.
Results may differ from a plain program's by a relative error of at most 0.015.
Values may be sent and summed in bfloat16 or wider, within the bound.
No kernel may reach another device: no remote copies, remote signals or barrier semaphores. Data moves between devices by JAX's collectives and lax.ppermute only.
A program may use at most 192 MiB of HBM per device.

v0:
```python
import functools
import math

import jax
import jax.numpy as jnp
import ml_dtypes
import numpy as np
from jax import lax
from jax.experimental import pallas as pl
from jax.experimental.pallas import tpu as pltpu
from jax.sharding import PartitionSpec as P

BOTH = ("dp", "space")
LANES = 128
WIDE = 3 * LANES
HALF = WIDE // 2
SPARE = 41
GUEST = 21
PAIRS = 5
MIB = 1024 * 1024
VMEM = 62 * MIB
ANY = pl.BlockSpec(memory_space=pl.ANY)


def lane_layout(start, freqs):
    lane = np.arange(WIDE)
    tail = lane >= 256
    imag = np.where(tail, lane >= 320, lane >= 128)
    freq = start + np.where(tail, 128 + lane % 64, lane % 128)
    return np.minimum(freq, freqs - 1), imag, freq < freqs


def row_tables(lon_len, start):
    freqs = lon_len // 2 + 1
    freq, imag, used = lane_layout(start, freqs)
    lon = np.arange(lon_len)
    turns = (lon[:, None] * freq[None, :] % lon_len).astype(np.float32) * np.float32(
        2.0 * math.pi / lon_len
    )
    scale = np.float32(1.0 / math.sqrt(lon_len))
    wave = np.where(imag, -np.sin(turns), np.cos(turns)) * used
    weight = np.where((freq == 0) | (freq == lon_len // 2), 1.0, 2.0).astype(np.float32)
    forward = (wave * scale).astype(ml_dtypes.bfloat16)
    inverse = (wave * weight * scale).astype(ml_dtypes.bfloat16)
    return forward.T, inverse


def guest_home(part):
    return part // 2 * 64 + part % 2 * GUEST


def guest_columns(table):
    guests = np.zeros((table.shape[0], 4 * LANES), table.dtype)
    for part in range(4):
        home = 2 * LANES + guest_home(part)
        width = min(GUEST, SPARE - part % 2 * GUEST)
        seat = part * LANES + SPARE
        guests[:, seat : seat + width] = table[:, home : home + width]
    return np.concatenate([table[:, : 2 * LANES], guests], axis=1)


def column_tables(spaces, rows, chan_part):
    lat_len = spaces * rows
    lat = np.arange(lat_len)
    turns = (lat[:, None] * lat[None, :] % lat_len).astype(np.float32) * np.float32(
        2.0 * math.pi / lat_len
    )
    scale = np.float32(1.0 / math.sqrt(lat_len))
    size = chan_part * lat_len
    order = lat.reshape(spaces, rows // 2, 2).transpose(1, 0, 2).reshape(-1)
    forward = np.zeros((chan_part, lat_len, 2, lat_len, chan_part), np.float32)
    for chan in range(chan_part):
        forward[chan, :, 0, :, chan] = (np.cos(turns) * scale)[:, order]
        forward[chan, :, 1, :, chan] = (np.sin(turns) * scale)[:, order]
    inverse = forward.transpose(3, 4, 2, 0, 1).reshape(size, 2 * size)
    forward = forward.reshape(size, 2 * size)
    return forward.astype(ml_dtypes.bfloat16), inverse.astype(ml_dtypes.bfloat16)


def swap_parts(values):
    tail = values[:, 2 * LANES :]
    return jnp.concatenate(
        [values[:, LANES : 2 * LANES], values[:, :LANES], pltpu.roll(tail, 64, axis=1)], axis=1
    )


def imag_lanes(shape):
    lane = lax.broadcasted_iota(jnp.int32, shape, len(shape) - 1)
    return ((lane >= LANES) & (lane < 2 * LANES)) | (lane >= 320)


def first_half(shape):
    return lax.broadcasted_iota(jnp.int32, shape, 1) < 4


def interleave(one, two):
    top = first_half(one.shape)
    return (
        jnp.where(top, one, pltpu.roll(two, 4, axis=1)),
        jnp.where(top, pltpu.roll(one, 4, axis=1), two),
    )


def normed_row(values, gain, bias):
    wide = values.astype(jnp.float32)
    center = jnp.mean(wide, axis=-1, keepdims=True)
    wide = wide - center
    spread = jnp.mean(jnp.square(wide), axis=-1, keepdims=True)
    return (wide * lax.rsqrt(spread + 1e-05) * gain + bias).astype(jnp.bfloat16)


def pair_spectra(x_ref, gain_ref, bias_ref, table):
    specs = []
    for row in range(2):
        normed = normed_row(x_ref[row], gain_ref[...], bias_ref[...])
        spec = jnp.dot(table, normed, preferred_element_type=jnp.float32).T
        specs.append(spec.reshape(spec.shape[0] // 8, 8, spec.shape[1]))
    return interleave(*specs)


def pre_kernel(x_ref, gain_ref, bias_ref, table_ref, out_ref):
    both = pair_spectra(x_ref, gain_ref, bias_ref, table_ref[...])
    for side in range(2):
        out_ref[:, side, 0] = both[side].astype(jnp.bfloat16)


def pre_packed_kernel(x_ref, gain_ref, bias_ref, table_ref, last_ref, out_ref):
    pair = pl.program_id(0)

    def main(both):
        for side in range(2):
            for tile in range(2):
                out_ref[:, side, 2 * pair + tile] = both[side][
                    :, :, tile * LANES : (tile + 1) * LANES
                ].astype(jnp.bfloat16)

    @pl.when(pair < PAIRS - 1)
    def _():
        both = pair_spectra(x_ref, gain_ref, bias_ref, table_ref[...])
        main(both)
        for side in range(2):
            out_ref[:, side, 2 * PAIRS + pair] = both[side][:, :, 2 * LANES :].astype(jnp.bfloat16)

    @pl.when(pair == PAIRS - 1)
    def _():
        both = pair_spectra(x_ref, gain_ref, bias_ref, last_ref[...])
        main(both)
        for side in range(2):
            for part in range(4):
                guest = both[side][:, :, (2 + part) * LANES : (3 + part) * LANES]
                tail = out_ref[:, side, 2 * PAIRS + part].astype(jnp.float32)
                out_ref[:, side, 2 * PAIRS + part] = (tail + guest).astype(jnp.bfloat16)


def pre(grid, gain, bias, table, packed):
    rows, lon_len, channels = grid.shape
    groups = channels // 8
    if packed:
        kernel = pre_packed_kernel
        shape = (groups, 2, 3 * PAIRS - 1, 8, LANES)
        out_spec = pl.BlockSpec(shape, lambda i: (0, 0, 0, 0, 0))
        tables = (table, guest_columns(table.T).T)
    else:
        kernel = pre_kernel
        shape = (groups, 2, PAIRS, 8, WIDE)
        out_spec = pl.BlockSpec((groups, 2, 1, 8, WIDE), lambda i: (0, 0, i, 0, 0))
        tables = (table,)
    out = pl.pallas_call(
        kernel,
        grid=(rows // 2,),
        in_specs=[
            pl.BlockSpec((2, lon_len, channels), lambda i: (i, 0, 0)),
            pl.BlockSpec((1, channels), lambda i: (0, 0)),
            pl.BlockSpec((1, channels), lambda i: (0, 0)),
        ]
        + [pl.BlockSpec(each.shape, lambda i: (0, 0)) for each in tables],
        out_specs=out_spec,
        out_shape=jax.ShapeDtypeStruct(shape, jnp.bfloat16),
        compiler_params=pltpu.CompilerParams(vmem_limit_bytes=VMEM),
        cost_estimate=pl.CostEstimate(
            flops=2 * rows * lon_len * channels * WIDE,
            bytes_accessed=2 * rows * channels * (lon_len + WIDE),
            transcendentals=rows * lon_len,
        ),
        name="row_forward",
    )(grid, gain, bias, *(jnp.asarray(each) for each in tables))
    return out.reshape(2 * groups, *shape[2:])


def guest_lanes(shape, first):
    lane = lax.broadcasted_iota(jnp.int32, shape, 1)
    return (lane >= first) & (lane < first + GUEST)


def load_pairs(x_ref, packed):
    pairs = []
    if not packed:
        for pair in range(PAIRS):
            rows = x_ref[:, pair].astype(jnp.float32)
            pairs.append(rows.reshape(rows.shape[0] * 8, WIDE))
        return pairs
    tiles = []
    for tile in range(3 * PAIRS - 1):
        rows = x_ref[:, tile].astype(jnp.float32)
        tiles.append(rows.reshape(rows.shape[0] * 8, LANES))
    tails = tiles[2 * PAIRS :]
    last = jnp.zeros_like(tails[0])
    for part in range(4):
        home = guest_home(part)
        moved = pltpu.roll(tails[part], (home - SPARE) % LANES, axis=1)
        last = jnp.where(guest_lanes(last.shape, home), moved, last)
    tails.append(last)
    for pair in range(PAIRS):
        pairs.append(jnp.concatenate([tiles[2 * pair], tiles[2 * pair + 1], tails[pair]], axis=1))
    return pairs


def store_pairs(out_ref, back, packed):
    count = back.shape[0] // PAIRS
    pairs = [back[pair * count : (pair + 1) * count] for pair in range(PAIRS)]
    if not packed:
        for pair in range(PAIRS):
            out_ref[:, pair] = pairs[pair].reshape(count // 8, 8, WIDE).astype(jnp.bfloat16)
        return
    tails = [rows[:, 2 * LANES :] for rows in pairs]
    for part in range(4):
        moved = pltpu.roll(tails[-1], (SPARE - guest_home(part)) % LANES, axis=1)
        tails[part] = jnp.where(guest_lanes(moved.shape, SPARE), moved, tails[part])
    tiles = []
    for rows in pairs:
        tiles += [rows[:, :LANES], rows[:, LANES : 2 * LANES]]
    for index, tile in enumerate(tiles + tails[:-1]):
        out_ref[:, index] = tile.reshape(count // 8, 8, LANES).astype(jnp.bfloat16)


def mid_kernel(packed, x_ref, filt_ref, forward_ref, inverse_ref, out_ref, x_both, mixed):
    size = x_both.shape[0] // 2
    count = size // PAIRS
    for pair, rows in enumerate(load_pairs(x_ref, packed)):
        turned = swap_parts(rows)
        x_both[pl.ds(pair * count, count)] = rows.astype(jnp.bfloat16)
        x_both[pl.ds(size + pair * count, count)] = jnp.where(
            imag_lanes(rows.shape), -turned, turned
        ).astype(jnp.bfloat16)
    lat_len = size // 4
    for chan in range(4):
        part = pl.ds(chan * lat_len, lat_len)
        spec = jnp.dot(forward_ref[part], x_both[...], preferred_element_type=jnp.float32)
        both = filt_ref[0, part] * spec + filt_ref[1, part] * swap_parts(spec)
        turned = swap_parts(both)
        mixed[part] = both.astype(jnp.bfloat16)
        mixed[pl.ds(size + chan * lat_len, lat_len)] = jnp.where(
            imag_lanes(both.shape), turned, -turned
        ).astype(jnp.bfloat16)
    back = jnp.dot(inverse_ref[...], mixed[...], preferred_element_type=jnp.float32)
    store_pairs(out_ref, back, packed)


def mid(slab, filt, forward, inverse, samples, packed):
    spaces = slab.shape[0] // samples
    size = forward.shape[0]
    block = pl.BlockSpec((spaces, *slab.shape[1:]), lambda s: (s, 0, 0, 0))
    once = pl.Buffered(1)
    return pl.pallas_call(
        functools.partial(mid_kernel, packed),
        grid=(samples,),
        in_specs=[
            block,
            pl.BlockSpec((2, size, WIDE), lambda s: (0, 0, 0), pipeline_mode=once),
            pl.BlockSpec((size, 2 * size), lambda s: (0, 0), pipeline_mode=once),
            pl.BlockSpec((size, 2 * size), lambda s: (0, 0), pipeline_mode=once),
        ],
        out_specs=block,
        out_shape=jax.ShapeDtypeStruct(slab.shape, jnp.bfloat16),
        scratch_shapes=[
            pltpu.VMEM((2 * size, WIDE), jnp.bfloat16),
            pltpu.VMEM((2 * size, WIDE), jnp.bfloat16),
        ],
        compiler_params=pltpu.CompilerParams(vmem_limit_bytes=VMEM),
        cost_estimate=pl.CostEstimate(
            flops=samples * 8 * size * size * WIDE,
            bytes_accessed=4 * samples * size * WIDE + 8 * size * (WIDE + size),
            transcendentals=0,
        ),
        name="columns",
    )(slab, filt, forward, inverse)


def post_kernel(packed, back_hbm, x_hbm, table, out_hbm, x_in, out, slab, spec, *sems):
    x_sem, out_sem, main_sem, tail_sem = sems
    groups = slab.shape[0]

    def inputs(pair):
        mains = pl.ds(2 * pair, 2) if packed else pair
        copies = [
            pltpu.make_async_copy(
                back_hbm.at[:, :, mains], slab.at[:, :, mains], main_sem.at[pair]
            )
        ]
        if packed and pair < PAIRS - 1:
            tail = 2 * PAIRS + pair
            copies.append(
                pltpu.make_async_copy(
                    back_hbm.at[:, :, tail], slab.at[:, :, tail], tail_sem.at[pair]
                )
            )
        copies.append(
            pltpu.make_async_copy(x_hbm.at[pl.ds(2 * pair, 2)], x_in.at[pair], x_sem.at[pair])
        )
        return copies

    def output(pair):
        return pltpu.make_async_copy(out.at[pair], out_hbm.at[pl.ds(2 * pair, 2)], out_sem.at[pair])

    def rows_of(tile):
        both = (slab[:, side, tile].astype(jnp.float32) for side in range(2))
        return [each.reshape(groups * 8, each.shape[2]) for each in interleave(*both)]

    def tail_rows(pair):
        if pair < PAIRS - 1:
            return rows_of(2 * PAIRS + pair)
        last = [jnp.zeros((groups * 8, LANES), jnp.float32)] * 2
        for part in range(4):
            home = guest_home(part)
            for row, guest in enumerate(rows_of(2 * PAIRS + part)):
                moved = pltpu.roll(guest, (home - SPARE) % LANES, axis=1)
                last[row] = jnp.where(guest_lanes(moved.shape, home), moved, last[row])
        return last

    for copy in inputs(0) + inputs(1):
        copy.start()
    for pair in range(PAIRS):
        for copy in inputs(pair):
            copy.wait()
        if pair + 2 < PAIRS:
            for copy in inputs(pair + 2):
                copy.start()
        if packed:
            tiles = [rows_of(2 * pair), rows_of(2 * pair + 1), tail_rows(pair)]
        else:
            tiles = [rows_of(pair)]
        for row in range(2):
            lane = 0
            for tile in tiles:
                wide = tile[row].shape[1]
                spec[row, :, lane : lane + wide] = tile[row].astype(jnp.bfloat16)
                lane += wide
        for row in range(2):
            branch = lax.dot_general(
                table[...], spec[row], (((1,), (1,)), ((), ())), preferred_element_type=jnp.float32
            )
            out[pair, row] = (x_in[pair, row].astype(jnp.float32) + branch).astype(jnp.bfloat16)
        output(pair).start()
    for pair in range(PAIRS):
        output(pair).wait()


def post(back, grid, table, packed):
    rows, lon_len, channels = grid.shape
    groups = channels // 8
    back = back.reshape(groups, 2, *back.shape[1:])
    return pl.pallas_call(
        functools.partial(post_kernel, packed),
        in_specs=[ANY, ANY, pl.BlockSpec(memory_space=pltpu.VMEM)],
        out_specs=ANY,
        out_shape=jax.ShapeDtypeStruct(grid.shape, jnp.bfloat16),
        scratch_shapes=[
            pltpu.VMEM((PAIRS, 2, lon_len, channels), jnp.bfloat16),
            pltpu.VMEM((PAIRS, 2, lon_len, channels), jnp.bfloat16),
            pltpu.VMEM(back.shape, jnp.bfloat16),
            pltpu.VMEM((2, channels, WIDE), jnp.bfloat16),
        ]
        + [pltpu.SemaphoreType.DMA((PAIRS,))] * 4,
        compiler_params=pltpu.CompilerParams(vmem_limit_bytes=VMEM - MIB),
        cost_estimate=pl.CostEstimate(
            flops=2 * rows * lon_len * channels * WIDE,
            bytes_accessed=2 * rows * channels * (2 * lon_len + WIDE),
            transcendentals=0,
        ),
        name="row_inverse",
    )(back, grid, jnp.asarray(table))


def filter_chunk(filt, start):
    freqs = filt.shape[-1] // 2
    by_chan = filt.transpose(1, 0, 2).reshape(-1, 2 * freqs)

    def lanes(first):
        stop = min(start + HALF, freqs)
        taken = by_chan[:, first + start : first + stop]
        return jnp.pad(taken, ((0, 0), (0, HALF - taken.shape[1])))

    real, imag = lanes(0), lanes(freqs)

    def lay(one, two):
        return jnp.concatenate(
            [one[:, :LANES], two[:, :LANES], one[:, LANES:], two[:, LANES:]], axis=1
        )

    return jnp.stack([lay(real, real), lay(-imag, imag)])


def swap_devices(blocks):
    return lax.all_to_all(blocks, BOTH, split_axis=0, concat_axis=0, tiled=True)


def shards(samples, norm_gain, norm_bias, spectral_filter):
    grid = samples[0]
    rows, lon_len, _ = grid.shape
    dp_count = lax.axis_size("dp")
    starts = (0, HALF)
    tables = [row_tables(lon_len, start) for start in starts]
    columns = column_tables(lax.axis_size("space"), rows, spectral_filter.shape[1])
    forward, inverse = (jnp.asarray(each) for each in columns)
    gain, bias = norm_gain[None], norm_bias[None]
    spectra = [pre(grid, gain, bias, tables[index][0], index == 1) for index in range(2)]
    filts = [filter_chunk(spectral_filter, start) for start in starts]
    spectra[1], filts = lax.optimization_barrier((spectra[1], filts))
    slabs = [swap_devices(each) for each in spectra]
    backs = []
    for index in range(2):
        back = mid(slabs[index], filts[index], forward, inverse, dp_count, index == 1)
        backs.append(swap_devices(back))
    for index in range(2):
        grid = post(backs[index], grid, tables[index][1], index == 1)
    return grid[None]


def solution(mesh):
    placed = (P("dp", "space", None, None), P(), P(), P(None, BOTH, None))
    return jax.shard_map(
        shards, mesh=mesh, in_specs=placed, out_specs=P("dp", "space", None, None), check_vma=False
    )
```

profile of v0, /device:TPU:14, one launch (start us, length us, event | category | flops | bytes accessed | tf_op | source)
XLA Modules:
  0.0 239.0 jit_solution(14731250476266210726)
XLA Ops:
  0.0 10.9 %row_forward.3 = bf16[64,2,5,8,384]{4,3,2,1,0:T(8,128)(2,1)} custom-call(bf16[10,720,512]{2,1,0:T(8,128)(2,1)} %bitcast.18, f32[1,512]{1,0:T(1,128)} %bitcast.28, f32[1,512]{1,0:T(1,128)} %bitcast.30, bf16[384,720]{1,0:T(8,128)(2,1)} %constant.19.clone.table_ref), custom_call_target="tpu_custom_call" | custom-call | flops 2831155200 | bytes 11304960 | tf_op jit(solution)/shard_map/row_forward/pallas_call | solution.py:168
  10.9 10.8 %all-to-all-start.2 = ((bf16[128,5,8,384]{3,2,1,0:T(8,128)(2,1)}), bf16[128,5,8,384]{3,2,1,0:T(8,128)(2,1)}, u32[]{:S(2)}, u32[]{:S(2)}) async-start(bf16[128,5,8,384]{3,2,1,0:T(8,128)(2,1)} %bitcast.25), calls=%async_computation.2 | async-start | bytes 7864320 | tf_op jit(solution)/shard_map/all_to_all | solution.py:404
  21.7 2.9 %copy.12 = f32[4,320,722]{2,1,0:T(8,128)S(1)} copy(f32[4,320,722]{2,0,1:T(4,128)} %bitcast.27) | data formatting | bytes 7393280 | tf_op jit(solution)/shard_map/transpose | solution.py:386
  24.6 1.8 fusion.3
  26.9 0.7 fusion.2
  27.7 0.9 slice.81
  28.6 0.9 pad_slice_fusion
  29.5 0.9 fusion
  30.4 12.8 %row_forward.2 = bf16[64,2,14,8,128]{4,3,2,1,0:T(8,128)(2,1)} custom-call(bf16[10,720,512]{2,1,0:T(8,128)(2,1)} %bitcast.19, f32[1,512]{1,0:T(1,128)} %bitcast.29, f32[1,512]{1,0:T(1,128)} %bitcast.31, bf16[384,720]{1,0:T(8,128)(2,1)} %constant.20.clone.table_ref, bf16[768,720]{1,0:T(8,128)(2,1)} %constant.21.clone.last_ref), custom_call_target="tpu_custom_call" | custom-call | flops 2831155200 | bytes 11304960 | tf_op jit(solution)/shard_map/row_forward/pallas_call | solution.py:168
  43.3 1.9 fusion.4
  46.5 0.7 copy-done.2
  48.0 2.2 pad_maximum_fusion.filt_ref
  50.7 2.2 pad_maximum_fusion.1.filt_ref
  52.9 16.2 %all-to-all-done.2.x_ref = bf16[128,5,8,384]{3,2,1,0:T(8,128)(2,1)} async-done(((bf16[128,5,8,384]{3,2,1,0:T(8,128)(2,1)}), bf16[128,5,8,384]{3,2,1,0:T(8,128)(2,1)}, u32[]{:S(2)}, u32[]{:S(2)}) %all-to-all-start.2) | async-done | bytes 3932192 | tf_op jit(solution)/shard_map/all_to_all | solution.py:404
  69.1 7.8 %all-to-all-start = ((bf16[128,14,8,128]{3,2,1,0:T(8,128)(2,1)}), bf16[128,14,8,128]{3,2,1,0:T(8,128)(2,1)}, u32[]{:S(2)}, u32[]{:S(2)}) async-start(bf16[128,14,8,128]{3,2,1,0:T(8,128)(2,1)} %bitcast.26), calls=%async_computation | async-start | bytes 7340032 | tf_op jit(solution)/shard_map/all_to_all | solution.py:404
  76.9 35.1 %columns.3 = bf16[128,5,8,384]{3,2,1,0:T(8,128)(2,1)} custom-call(bf16[128,5,8,384]{3,2,1,0:T(8,128)(2,1)} %all-to-all-done.2.x_ref, f32[2,1280,384]{2,1,0:T(8,128)} %pad_maximum_fusion.filt_ref, bf16[1280,2560]{1,0:T(8,128)(2,1)} %constant.17.clone.forward_ref, bf16[1280,2560]{1,0:T(8,128)(2,1)} %constant.18.clone.inverse_ref), custom_call_target="tpu_custom_call" | custom-call | flops 20132659200 | bytes 24903680 | tf_op jit(solution)/shard_map/columns/pallas_call | solution.py:264
  112.0 9.4 %all-to-all-done.x_ref = bf16[128,14,8,128]{3,2,1,0:T(8,128)(2,1)} async-done(((bf16[128,14,8,128]{3,2,1,0:T(8,128)(2,1)}), bf16[128,14,8,128]{3,2,1,0:T(8,128)(2,1)}, u32[]{:S(2)}, u32[]{:S(2)}) %all-to-all-start) | async-done | bytes 3670048 | tf_op jit(solution)/shard_map/all_to_all | solution.py:404
  121.4 7.6 %all-to-all-start.3 = ((bf16[128,5,8,384]{3,2,1,0:T(8,128)(2,1)}), bf16[128,5,8,384]{3,2,1,0:T(8,128)(2,1)}, u32[]{:S(2)}, u32[]{:S(2)}) async-start(bf16[128,5,8,384]{3,2,1,0:T(8,128)(2,1)} %columns.3), calls=%async_computation.3 | async-start | bytes 7864320 | tf_op jit(solution)/shard_map/all_to_all | solution.py:404
  129.0 35.4 %columns.2 = bf16[128,14,8,128]{3,2,1,0:T(8,128)(2,1)} custom-call(bf16[128,14,8,128]{3,2,1,0:T(8,128)(2,1)} %all-to-all-done.x_ref, f32[2,1280,384]{2,1,0:T(8,128)} %pad_maximum_fusion.1.filt_ref, bf16[1280,2560]{1,0:T(8,128)(2,1)} %constant.17.clone.forward_ref, bf16[1280,2560]{1,0:T(8,128)(2,1)} %constant.18.clone.inverse_ref), custom_call_target="tpu_custom_call" | custom-call | flops 20132659200 | bytes 24903680 | tf_op jit(solution)/shard_map/columns/pallas_call | solution.py:264
  164.5 12.0 %all-to-all-done.3 = bf16[128,5,8,384]{3,2,1,0:T(8,128)(2,1)} async-done(((bf16[128,5,8,384]{3,2,1,0:T(8,128)(2,1)}), bf16[128,5,8,384]{3,2,1,0:T(8,128)(2,1)}, u32[]{:S(2)}, u32[]{:S(2)}) %all-to-all-start.3) | async-done | bytes 3932192 | tf_op jit(solution)/shard_map/all_to_all | solution.py:404
  176.5 7.8 %all-to-all-start.1 = ((bf16[128,14,8,128]{3,2,1,0:T(8,128)(2,1)}), bf16[128,14,8,128]{3,2,1,0:T(8,128)(2,1)}, u32[]{:S(2)}, u32[]{:S(2)}) async-start(bf16[128,14,8,128]{3,2,1,0:T(8,128)(2,1)} %columns.2), calls=%async_computation.1 | async-start | bytes 7340032 | tf_op jit(solution)/shard_map/all_to_all | solution.py:404
  184.3 10.0 %row_inverse.2.x_hbm = bf16[10,720,512]{2,1,0:T(8,128)(2,1)} custom-call(bf16[64,2,5,8,384]{4,3,2,1,0:T(8,128)(2,1)} %bitcast.12.back_hbm, bf16[10,720,512]{2,1,0:T(8,128)(2,1)} %bitcast.20, bf16[720,384]{1,0:T(8,128)(2,1)} %constant.22.clone.table), custom_call_target="tpu_custom_call" | custom-call | flops 2831155200 | bytes 18677760 | tf_op jit(solution)/shard_map/row_inverse/pallas_call | solution.py:362
  194.2 34.5 %all-to-all-done.1 = bf16[128,14,8,128]{3,2,1,0:T(8,128)(2,1)} async-done(((bf16[128,14,8,128]{3,2,1,0:T(8,128)(2,1)}), bf16[128,14,8,128]{3,2,1,0:T(8,128)(2,1)}, u32[]{:S(2)}, u32[]{:S(2)}) %all-to-all-start.1) | async-done | bytes 3670048 | tf_op jit(solution)/shard_map/all_to_all | solution.py:404
  228.8 10.1 %row_inverse.3 = bf16[10,720,512]{2,1,0:T(8,128)(2,1)} custom-call(bf16[64,2,14,8,128]{4,3,2,1,0:T(8,128)(2,1)} %bitcast.10.back_hbm, bf16[10,720,512]{2,1,0:T(8,128)(2,1)} %row_inverse.2.x_hbm, bf16[720,384]{1,0:T(8,128)(2,1)} %constant.23.clone.table), custom_call_target="tpu_custom_call" | custom-call | flops 2831155200 | bytes 18677760 | tf_op jit(solution)/shard_map/row_inverse/pallas_call | solution.py:362
  (16 shorter events, 3.1 us)
Async XLA Ops:
  10.9 58.2 %all-to-all-start.2 = ((bf16[128,5,8,384]{3,2,1,0:T(8,128)(2,1)}), bf16[128,5,8,384]{3,2,1,0:T(8,128)(2,1)}, u32[]{:S(2)}, u32[]{:S(2)}) async-start(bf16[128,5,8,384]{3,2,1,0:T(8,128)(2,1)} %bitcast.25), calls=%async_computation.2 | async-start | bytes 7864320 | tf_op jit(solution)/shard_map/all_to_all | solution.py:404
  24.6 2.4 copy-start
  43.2 2.7 %copy-start.1 = (f32[4,320,722]{2,1,0:T(8,128)S(1)}, f32[4,320,722]{2,1,0:T(8,128)}, u32[]{:S(2)}) copy-start(f32[4,320,722]{2,1,0:T(8,128)} %copy-done) | copy-start | bytes 11089924
  46.0 1.3 copy-start.2
  46.0 1.5 copy-start.3
  48.0 2.2 copy-start.4
  48.0 2.2 copy-start.5
  69.1 52.3 %all-to-all-start = ((bf16[128,14,8,128]{3,2,1,0:T(8,128)(2,1)}), bf16[128,14,8,128]{3,2,1,0:T(8,128)(2,1)}, u32[]{:S(2)}, u32[]{:S(2)}) async-start(bf16[128,14,8,128]{3,2,1,0:T(8,128)(2,1)} %bitcast.26), calls=%async_computation | async-start | bytes 7340032 | tf_op jit(solution)/shard_map/all_to_all | solution.py:404
  121.4 55.0 %all-to-all-start.3 = ((bf16[128,5,8,384]{3,2,1,0:T(8,128)(2,1)}), bf16[128,5,8,384]{3,2,1,0:T(8,128)(2,1)}, u32[]{:S(2)}, u32[]{:S(2)}) async-start(bf16[128,5,8,384]{3,2,1,0:T(8,128)(2,1)} %columns.3), calls=%async_computation.3 | async-start | bytes 7864320 | tf_op jit(solution)/shard_map/all_to_all | solution.py:404
  176.5 52.3 %all-to-all-start.1 = ((bf16[128,14,8,128]{3,2,1,0:T(8,128)(2,1)}), bf16[128,14,8,128]{3,2,1,0:T(8,128)(2,1)}, u32[]{:S(2)}, u32[]{:S(2)}) async-start(bf16[128,14,8,128]{3,2,1,0:T(8,128)(2,1)} %columns.2), calls=%async_computation.1 | async-start | bytes 7340032 | tf_op jit(solution)/shard_map/all_to_all | solution.py:404
where the time goes:
time: 242 us; the launch traced here: 239 us
  Pallas kernels  114 us (47%)
  waiting for transfers between devices  72.2 us (30%)
  starting transfers between devices  33.9 us (14%)
  local copies, waits for them, and re-layouts  10.1 us (4%)
  other arithmetic  8.23 us (3%)
    all_to_all x4, waiting for transfers between devices, swap_devices(): return lax.all_to_all(blocks, BOTH, split_axis=0, concat_axis=0, tiled=True)  72.2 us
    pallas_call x2, Pallas kernels, mid(): pl.pallas_call(functools.partial(mid_kernel, packed), grid=(samples,), in...  70.5 us
    all_to_all x4, starting transfers between devices, swap_devices(): return lax.all_to_all(blocks, BOTH, split_axis=0, concat_axis=0, tiled=True)  33.9 us
    pallas_call x2, Pallas kernels, pre(): pl.pallas_call(kernel, grid=(rows // 2,), in_specs=[pl.BlockSpec((2, lon_...  23.7 us
    pallas_call x2, Pallas kernels, post(): pl.pallas_call(functools.partial(post_kernel, packed), in_specs=[ANY, ANY...  20 us
    another operation x4, other arithmetic, filter_chunk(): return jnp.stack([lay(real, real), lay(-imag, imag)])  5.4 us
  transfers between devices with their start and end apart: 4, of which 4 were waited for; matrix products, arithmetic and copies ran while one was open for 7% of the time, Pallas kernels for 39%

commit v1 on v0

--- a/solution.py
+++ b/solution.py
@@ -286,9 +286,10 @@
     )(slab, filt, forward, inverse)
 
 
-def post_kernel(packed, back_hbm, x_hbm, table, out_hbm, x_in, out, slab, spec, *sems):
-    x_sem, out_sem, main_sem, tail_sem = sems
+def post_kernel(packed, back_hbm, x_hbm, table_hbm, out_hbm, x_in, out, slab, spec, table, *sems):
+    x_sem, out_sem, main_sem, tail_sem, table_sem = sems
     groups = slab.shape[0]
+    tables = pltpu.make_async_copy(table_hbm, table, table_sem)
 
     def inputs(pair):
         mains = pl.ds(2 * pair, 2) if packed else pair
@@ -327,11 +328,13 @@
                 last[row] = jnp.where(guest_lanes(moved.shape, home), moved, last[row])
         return last
 
-    for copy in inputs(0) + inputs(1):
+    for copy in [tables] + inputs(0) + inputs(1):
         copy.start()
     for pair in range(PAIRS):
         for copy in inputs(pair):
             copy.wait()
+        if pair == 0:
+            tables.wait()
         if pair + 2 < PAIRS:
             for copy in inputs(pair + 2):
                 copy.start()
@@ -361,7 +364,7 @@
     back = back.reshape(groups, 2, *back.shape[1:])
     return pl.pallas_call(
         functools.partial(post_kernel, packed),
-        in_specs=[ANY, ANY, pl.BlockSpec(memory_space=pltpu.VMEM)],
+        in_specs=[ANY] * 3,
         out_specs=ANY,
         out_shape=jax.ShapeDtypeStruct(grid.shape, jnp.bfloat16),
         scratch_shapes=[
@@ -369,8 +372,10 @@
             pltpu.VMEM((PAIRS, 2, lon_len, channels), jnp.bfloat16),
             pltpu.VMEM(back.shape, jnp.bfloat16),
             pltpu.VMEM((2, channels, WIDE), jnp.bfloat16),
+            pltpu.VMEM((lon_len, WIDE), jnp.bfloat16),
         ]
-        + [pltpu.SemaphoreType.DMA((PAIRS,))] * 4,
+        + [pltpu.SemaphoreType.DMA((PAIRS,))] * 4
+        + [pltpu.SemaphoreType.DMA],
         compiler_params=pltpu.CompilerParams(vmem_limit_bytes=VMEM - MIB),
         cost_estimate=pl.CostEstimate(
             flops=2 * rows * lon_len * channels * WIDE,

time: 242 us -> 241 us (level)
  no operation moved by 1% of the time
where the time goes in v1:
time: 241 us; the launch traced here: 238 us
  Pallas kernels  113 us (47%)
  waiting for transfers between devices  73.1 us (30%)
  starting transfers between devices  33.9 us (14%)
  local copies, waits for them, and re-layouts  10.1 us (4%)
  other arithmetic  8.23 us (3%)
    all_to_all x4, waiting for transfers between devices, swap_devices(): return lax.all_to_all(blocks, BOTH, split_axis=0, concat_axis=0, tiled=True)  73.1 us
    pallas_call x2, Pallas kernels, mid(): pl.pallas_call(functools.partial(mid_kernel, packed), grid=(samples,), in...  70.5 us
    all_to_all x4, starting transfers between devices, swap_devices(): return lax.all_to_all(blocks, BOTH, split_axis=0, concat_axis=0, tiled=True)  33.9 us
    pallas_call x2, Pallas kernels, pre(): pl.pallas_call(kernel, grid=(rows // 2,), in_specs=[pl.BlockSpec((2, lon_...  23.7 us
    pallas_call x2, Pallas kernels, post(): pl.pallas_call(functools.partial(post_kernel, packed), in_specs=[ANY] * 3...  18.3 us
    another operation x4, other arithmetic, filter_chunk(): return jnp.stack([lay(real, real), lay(-imag, imag)])  5.4 us
  transfers between devices with their start and end apart: 4, of which 4 were waited for; matrix products, arithmetic and copies ran while one was open for 7% of the time, Pallas kernels for 39%

profile of v1, /device:TPU:14, one launch (start us, length us, event | category | flops | bytes accessed | tf_op | source)
XLA Modules:
  0.0 238.2 jit_solution(12635644098582835023)
XLA Ops:
  0.0 10.9 %row_forward.3 = bf16[64,2,5,8,384]{4,3,2,1,0:T(8,128)(2,1)} custom-call(bf16[10,720,512]{2,1,0:T(8,128)(2,1)} %bitcast.18, f32[1,512]{1,0:T(1,128)} %bitcast.28, f32[1,512]{1,0:T(1,128)} %bitcast.30, bf16[384,720]{1,0:T(8,128)(2,1)} %constant.19.clone.table_ref), custom_call_target="tpu_custom_call" | custom-call | flops 2831155200 | bytes 11304960 | tf_op jit(solution)/shard_map/row_forward/pallas_call | solution.py:168
  10.9 10.8 %all-to-all-start.2 = ((bf16[128,5,8,384]{3,2,1,0:T(8,128)(2,1)}), bf16[128,5,8,384]{3,2,1,0:T(8,128)(2,1)}, u32[]{:S(2)}, u32[]{:S(2)}) async-start(bf16[128,5,8,384]{3,2,1,0:T(8,128)(2,1)} %bitcast.25), calls=%async_computation.2 | async-start | bytes 7864320 | tf_op jit(solution)/shard_map/all_to_all | solution.py:409
  21.7 2.9 %copy.12 = f32[4,320,722]{2,1,0:T(8,128)S(1)} copy(f32[4,320,722]{2,0,1:T(4,128)} %bitcast.27) | data formatting | bytes 7393280 | tf_op jit(solution)/shard_map/transpose | solution.py:391
  24.6 1.8 fusion.3
  26.9 0.7 fusion.2
  27.7 0.9 slice.81
  28.6 0.9 pad_slice_fusion
  29.5 0.9 fusion
  30.4 12.8 %row_forward.2 = bf16[64,2,14,8,128]{4,3,2,1,0:T(8,128)(2,1)} custom-call(bf16[10,720,512]{2,1,0:T(8,128)(2,1)} %bitcast.19, f32[1,512]{1,0:T(1,128)} %bitcast.29, f32[1,512]{1,0:T(1,128)} %bitcast.31, bf16[384,720]{1,0:T(8,128)(2,1)} %constant.20.clone.table_ref, bf16[768,720]{1,0:T(8,128)(2,1)} %constant.21.clone.last_ref), custom_call_target="tpu_custom_call" | custom-call | flops 2831155200 | bytes 11304960 | tf_op jit(solution)/shard_map/row_forward/pallas_call | solution.py:168
  43.3 1.9 fusion.4
  46.5 0.7 copy-done.2
  48.0 2.2 pad_maximum_fusion.filt_ref
  50.7 2.2 pad_maximum_fusion.1.filt_ref
  52.9 16.2 %all-to-all-done.2.x_ref = bf16[128,5,8,384]{3,2,1,0:T(8,128)(2,1)} async-done(((bf16[128,5,8,384]{3,2,1,0:T(8,128)(2,1)}), bf16[128,5,8,384]{3,2,1,0:T(8,128)(2,1)}, u32[]{:S(2)}, u32[]{:S(2)}) %all-to-all-start.2) | async-done | bytes 3932192 | tf_op jit(solution)/shard_map/all_to_all | solution.py:409
  69.1 7.8 %all-to-all-start = ((bf16[128,14,8,128]{3,2,1,0:T(8,128)(2,1)}), bf16[128,14,8,128]{3,2,1,0:T(8,128)(2,1)}, u32[]{:S(2)}, u32[]{:S(2)}) async-start(bf16[128,14,8,128]{3,2,1,0:T(8,128)(2,1)} %bitcast.26), calls=%async_computation | async-start | bytes 7340032 | tf_op jit(solution)/shard_map/all_to_all | solution.py:409
  76.9 35.1 %columns.3 = bf16[128,5,8,384]{3,2,1,0:T(8,128)(2,1)} custom-call(bf16[128,5,8,384]{3,2,1,0:T(8,128)(2,1)} %all-to-all-done.2.x_ref, f32[2,1280,384]{2,1,0:T(8,128)} %pad_maximum_fusion.filt_ref, bf16[1280,2560]{1,0:T(8,128)(2,1)} %constant.17.clone.forward_ref, bf16[1280,2560]{1,0:T(8,128)(2,1)} %constant.18.clone.inverse_ref), custom_call_target="tpu_custom_call" | custom-call | flops 20132659200 | bytes 24903680 | tf_op jit(solution)/shard_map/columns/pallas_call | solution.py:264
  112.0 9.4 %all-to-all-done.x_ref = bf16[128,14,8,128]{3,2,1,0:T(8,128)(2,1)} async-done(((bf16[128,14,8,128]{3,2,1,0:T(8,128)(2,1)}), bf16[128,14,8,128]{3,2,1,0:T(8,128)(2,1)}, u32[]{:S(2)}, u32[]{:S(2)}) %all-to-all-start) | async-done | bytes 3670048 | tf_op jit(solution)/shard_map/all_to_all | solution.py:409
  121.4 7.6 %all-to-all-start.3 = ((bf16[128,5,8,384]{3,2,1,0:T(8,128)(2,1)}), bf16[128,5,8,384]{3,2,1,0:T(8,128)(2,1)}, u32[]{:S(2)}, u32[]{:S(2)}) async-start(bf16[128,5,8,384]{3,2,1,0:T(8,128)(2,1)} %columns.3), calls=%async_computation.3 | async-start | bytes 7864320 | tf_op jit(solution)/shard_map/all_to_all | solution.py:409
  129.0 35.4 %columns.2 = bf16[128,14,8,128]{3,2,1,0:T(8,128)(2,1)} custom-call(bf16[128,14,8,128]{3,2,1,0:T(8,128)(2,1)} %all-to-all-done.x_ref, f32[2,1280,384]{2,1,0:T(8,128)} %pad_maximum_fusion.1.filt_ref, bf16[1280,2560]{1,0:T(8,128)(2,1)} %constant.17.clone.forward_ref, bf16[1280,2560]{1,0:T(8,128)(2,1)} %constant.18.clone.inverse_ref), custom_call_target="tpu_custom_call" | custom-call | flops 20132659200 | bytes 24903680 | tf_op jit(solution)/shard_map/columns/pallas_call | solution.py:264
  164.5 12.0 %all-to-all-done.3 = bf16[128,5,8,384]{3,2,1,0:T(8,128)(2,1)} async-done(((bf16[128,5,8,384]{3,2,1,0:T(8,128)(2,1)}), bf16[128,5,8,384]{3,2,1,0:T(8,128)(2,1)}, u32[]{:S(2)}, u32[]{:S(2)}) %all-to-all-start.3) | async-done | bytes 3932192 | tf_op jit(solution)/shard_map/all_to_all | solution.py:409
  176.5 7.8 %all-to-all-start.1 = ((bf16[128,14,8,128]{3,2,1,0:T(8,128)(2,1)}), bf16[128,14,8,128]{3,2,1,0:T(8,128)(2,1)}, u32[]{:S(2)}, u32[]{:S(2)}) async-start(bf16[128,14,8,128]{3,2,1,0:T(8,128)(2,1)} %columns.2), calls=%async_computation.1 | async-start | bytes 7340032 | tf_op jit(solution)/shard_map/all_to_all | solution.py:409
  184.3 9.0 %row_inverse.2.x_hbm = bf16[10,720,512]{2,1,0:T(8,128)(2,1)} custom-call(bf16[64,2,5,8,384]{4,3,2,1,0:T(8,128)(2,1)} %bitcast.12.back_hbm, bf16[10,720,512]{2,1,0:T(8,128)(2,1)} %bitcast.20, bf16[720,384]{1,0:T(8,128)(2,1)} %constant.22.clone.table_hbm), custom_call_target="tpu_custom_call" | custom-call | flops 2831155200 | bytes 18677760 | tf_op jit(solution)/shard_map/row_inverse/pallas_call | solution.py:365
  193.3 35.5 %all-to-all-done.1 = bf16[128,14,8,128]{3,2,1,0:T(8,128)(2,1)} async-done(((bf16[128,14,8,128]{3,2,1,0:T(8,128)(2,1)}), bf16[128,14,8,128]{3,2,1,0:T(8,128)(2,1)}, u32[]{:S(2)}, u32[]{:S(2)}) %all-to-all-start.1) | async-done | bytes 3670048 | tf_op jit(solution)/shard_map/all_to_all | solution.py:409
  228.8 9.3 %row_inverse.3 = bf16[10,720,512]{2,1,0:T(8,128)(2,1)} custom-call(bf16[64,2,14,8,128]{4,3,2,1,0:T(8,128)(2,1)} %bitcast.10.back_hbm, bf16[10,720,512]{2,1,0:T(8,128)(2,1)} %row_inverse.2.x_hbm, bf16[720,384]{1,0:T(8,128)(2,1)} %constant.23.clone.table_hbm), custom_call_target="tpu_custom_call" | custom-call | flops 2831155200 | bytes 18677760 | tf_op jit(solution)/shard_map/row_inverse/pallas_call | solution.py:365
  (16 shorter events, 3.1 us)
Async XLA Ops:
  10.9 58.2 %all-to-all-start.2 = ((bf16[128,5,8,384]{3,2,1,0:T(8,128)(2,1)}), bf16[128,5,8,384]{3,2,1,0:T(8,128)(2,1)}, u32[]{:S(2)}, u32[]{:S(2)}) async-start(bf16[128,5,8,384]{3,2,1,0:T(8,128)(2,1)} %bitcast.25), calls=%async_computation.2 | async-start | bytes 7864320 | tf_op jit(solution)/shard_map/all_to_all | solution.py:409
  24.6 2.4 copy-start
  43.2 2.7 %copy-start.1 = (f32[4,320,722]{2,1,0:T(8,128)S(1)}, f32[4,320,722]{2,1,0:T(8,128)}, u32[]{:S(2)}) copy-start(f32[4,320,722]{2,1,0:T(8,128)} %copy-done) | copy-start | bytes 11089924
  46.0 1.3 copy-start.2
  46.0 1.5 copy-start.3
  48.0 2.2 copy-start.4
  48.0 2.2 copy-start.5
  69.1 52.3 %all-to-all-start = ((bf16[128,14,8,128]{3,2,1,0:T(8,128)(2,1)}), bf16[128,14,8,128]{3,2,1,0:T(8,128)(2,1)}, u32[]{:S(2)}, u32[]{:S(2)}) async-start(bf16[128,14,8,128]{3,2,1,0:T(8,128)(2,1)} %bitcast.26), calls=%async_computation | async-start | bytes 7340032 | tf_op jit(solution)/shard_map/all_to_all | solution.py:409
  121.4 55.0 %all-to-all-start.3 = ((bf16[128,5,8,384]{3,2,1,0:T(8,128)(2,1)}), bf16[128,5,8,384]{3,2,1,0:T(8,128)(2,1)}, u32[]{:S(2)}, u32[]{:S(2)}) async-start(bf16[128,5,8,384]{3,2,1,0:T(8,128)(2,1)} %columns.3), calls=%async_computation.3 | async-start | bytes 7864320 | tf_op jit(solution)/shard_map/all_to_all | solution.py:409
  176.5 52.3 %all-to-all-start.1 = ((bf16[128,14,8,128]{3,2,1,0:T(8,128)(2,1)}), bf16[128,14,8,128]{3,2,1,0:T(8,128)(2,1)}, u32[]{:S(2)}, u32[]{:S(2)}) async-start(bf16[128,14,8,128]{3,2,1,0:T(8,128)(2,1)} %columns.2), calls=%async_computation.1 | async-start | bytes 7340032 | tf_op jit(solution)/shard_map/all_to_all | solution.py:409
